TPU v7x, 256 devices: a whole 4x4x8 slice. The times are simulated.
256 devices in a mesh: dp: 16 (over x, y_hi, core), mp: 16 (over y_lo, z).
Axes of the slice: x: 4, y: 4 (y_hi: 2, y_lo: 2; y = y_hi * 2 + y_lo), z: 8, core: 2. Of those that a mesh axis runs over, the one named last changes fastest.
Arguments:
- out_grads: bfloat16 [2048, 8192], P('dp', 'mp'), may hold values from -6 to 6
- basis: bfloat16 [8192, 8192], P('dp', 'mp'), may hold values from -0.0625 to 0.0625
- left_factors: bfloat16 [8192, 4096], P('mp', 'dp'), may hold values from -0.0625 to 0.0625
- right_factors: bfloat16 [28672, 4096], P('mp', 'dp'), may hold values from -0.03125 to 0.03125
- activations: bfloat16 [2048, 28672], P('dp', 'mp'), may hold values from -6 to 6
- spans: int32 [16, 5], P('dp'), may hold values from 1 to 64, 128 in all within a row
Outputs:
- scores: float32 [64, 128], P('dp', 'mp')
Inputs may be any that keep to these rules, and one draw needn't show every extreme that they name: `spans`: each row sums to 128; every entry is at least 1, and the largest entry of each row is exactly 64.
All inputs are finite; a program needn't handle non-finite values.
Results may differ from a plain program's by a relative error of at most 0.0029.
Values may be sent and summed in bfloat16 or wider, within the bound.
A program may use at most 128 MiB of HBM per device.

v0:
```python
import jax
import jax.numpy as jnp
from jax import lax
from jax.sharding import PartitionSpec as P

RANK = 32
TOK_DEV = 128
SEQ_DEV = 4


def on_device(out_grads, basis, left_factors, right_factors, activations, spans):
    tok_rows = out_grads.shape[0]
    grads_full = lax.all_gather(out_grads, "mp", axis=1, tiled=True)
    rotated = jnp.dot(
        grads_full,
        lax.all_gather(basis, "dp", axis=0, tiled=True),
        preferred_element_type=jnp.float32,
    ).astype(jnp.bfloat16)
    left_part = jnp.dot(
        rotated,
        lax.all_gather(left_factors, "dp", axis=1, tiled=True),
        preferred_element_type=jnp.float32,
    )
    right_part = jnp.dot(
        activations,
        lax.all_gather(right_factors, "dp", axis=1, tiled=True),
        preferred_element_type=jnp.float32,
    )
    left_sum, right_sum = (
        lax.psum_scatter(left_part, "mp", scatter_dimension=1, tiled=True),
        lax.psum_scatter(right_part, "mp", scatter_dimension=1, tiled=True),
    )
    queries = left_sum.shape[1] // RANK
    per_token = (left_sum * right_sum).reshape(tok_rows, queries, RANK).sum(axis=2)
    lengths = spans[0, :SEQ_DEV]
    starts = jnp.cumsum(spans[0])[:SEQ_DEV] - lengths
    slots = jnp.arange(tok_rows, dtype=jnp.int32)
    inside = (slots[None, :] >= starts[:, None]) & (slots[None, :] < (starts + lengths)[:, None])
    members = inside.astype(jnp.float32)
    summed = jnp.dot(
        members, per_token, precision=lax.Precision.HIGHEST, preferred_element_type=jnp.float32
    )
    scale = 1.0 / jnp.sqrt(jnp.float32(RANK * TOK_DEV))
    return summed * scale


def solution(mesh):
    placed = (
        P("dp", "mp"),
        P("dp", "mp"),
        P("mp", "dp"),
        P("mp", "dp"),
        P("dp", "mp"),
        P("dp", None),
    )
    return jax.shard_map(
        on_device, mesh=mesh, in_specs=placed, out_specs=P("dp", "mp"), check_vma=False
    )
```

profile of v0, /device:TPU:8, one launch (start us, length us, event | category | flops | bytes accessed | tf_op | source)
XLA Modules:
  0.0 500.3 jit_solution(11643034267215393919)
XLA Ops:
  6.5 0.7 all-gather.5.cloned.1.call-update
  7.3 0.0 all-gather.9.cloned.1.call-start
  7.3 0.7 all-gather.9.cloned.1.call-update
  8.0 0.0 all-gather.7.cloned.1.call-start
  8.1 0.7 all-gather.7.cloned.1.call-update
  8.7 0.0 all-gather.11.cloned.1.call-start
  8.8 0.5 all-gather.11.cloned.1.call-update
  9.3 0.0 reduce-scatter.3.cloned.1.call-start
  9.4 73.3 %all-gather.5.cloned.1.call-done = bf16[128,8192]{1,0:T(8,128)(2,1)} async-done(((bf16[128,512]{1,0:T(8,128)(2,1)}), bf16[128,8192]{1,0:T(8,128)(2,1)}) %all-gather.5.cloned.1.call-update) | async-done | bytes 2097168 | tf_op jit(solution)/shard_map/all_gather | solution.py:13
  82.6 64.1 %all-gather.9.cloned.1.call-done = bf16[512,4096]{1,0:T(8,128)(2,1)} async-done(((bf16[512,256]{1,0:T(8,128)(2,1)}), bf16[512,4096]{1,0:T(8,128)(2,1)}) %all-gather.9.cloned.1.call-update) | async-done | bytes 4194320 | tf_op jit(solution)/shard_map/all_gather | solution.py:21
  146.7 79.3 %all-gather.7.cloned.1.call-done = bf16[8192,512]{1,0:T(8,128)(2,1)} async-done(((bf16[512,512]{1,0:T(8,128)(2,1)}), bf16[8192,512]{1,0:T(8,128)(2,1)}) %all-gather.7.cloned.1.call-update) | async-done | bytes 8388624 | tf_op jit(solution)/shard_map/all_gather | solution.py:16
  226.0 8.4 %fusion = f32[128,4096]{1,0:T(8,128)} fusion(bf16[512,4096]{1,0:T(8,128)(2,1)} %all-gather.9.cloned.1.call-done, bf16[128,8192]{1,0:T(8,128)(2,1)} %all-gather.5.cloned.1.call-done, bf16[8192,512]{1,0:T(8,128)(2,1)} %all-gather.7.cloned.1.call-done), kind=kOutput, calls=%fused_computation.2 | convolution fusion | flops 1610678272 | bytes 16777216 | tf_op jit(solution)/shard_map/dot_general | solution.py:19
  234.4 0.0 reduce-scatter.3.cloned.1.call-update
  234.5 0.0 copy-start.1
  234.5 0.0 reduce-scatter.5.cloned.1.call-start
  234.5 109.3 %all-gather.11.cloned.1.call-done = bf16[1792,4096]{1,0:T(8,128)(2,1)} async-done(((bf16[1792,256]{1,0:T(8,128)(2,1)}), bf16[1792,4096]{1,0:T(8,128)(2,1)}) %all-gather.11.cloned.1.call-update) | async-done | bytes 14680080 | tf_op jit(solution)/shard_map/all_gather | solution.py:26
  343.9 8.5 %fusion.6 = f32[128,4096]{1,0:T(8,128)} fusion(bf16[128,1792]{1,0:T(8,128)(2,1)S(1)} %copy-done, bf16[1792,4096]{1,0:T(8,128)(2,1)} %all-gather.11.cloned.1.call-done), kind=kOutput, calls=%fused_computation.12 | convolution fusion | flops 1879048192 | bytes 17235968 | tf_op jit(solution)/shard_map/dot_general | solution.py:24
  352.4 0.0 reduce-scatter.5.cloned.1.call-update
  352.4 0.2 reduce-window.4
  352.6 66.2 %reduce-scatter.3.cloned.1.call-done = f32[128,256]{1,0:T(8,128)} async-done(((f32[128,4096]{1,0:T(8,128)}), f32[128,256]{1,0:T(8,128)}) %reduce-scatter.3.cloned.1.call-update) | async-done | bytes 131088 | tf_op jit(solution)/shard_map/reduce_scatter | solution.py:30
  418.8 72.8 %reduce-scatter.5.cloned.1.call-done = f32[128,256]{1,0:T(8,128)} async-done(((f32[128,4096]{1,0:T(8,128)}), f32[128,256]{1,0:T(8,128)}) %reduce-scatter.5.cloned.1.call-update) | async-done | bytes 131088 | tf_op jit(solution)/shard_map/reduce_scatter | solution.py:31
  491.6 1.0 mul.9
  492.6 0.1 copy.8
  492.7 0.8 convolution_multiply_fusion
  (6 shorter events, 0.0 us)
Async XLA Ops:
  6.5 337.3 %copy-start = (bf16[128,1792]{1,0:T(8,128)(2,1)S(1)}, bf16[128,1792]{1,0:T(8,128)(2,1)}, u32[]{:S(2)}) copy-start(bf16[128,1792]{1,0:T(8,128)(2,1)} %param.10) | copy-start | bytes 1376260
  6.5 76.1 %all-gather.5.cloned.1.call-start = ((), (), s32[]{:S(2)}) async-start(), calls=%async_computation.2 | async-start | bytes 2228224 | tf_op jit(solution)/shard_map/all_gather | solution.py:13
  7.3 139.5 %all-gather.9.cloned.1.call-start = ((), (), s32[]{:S(2)}) async-start(), calls=%async_computation.4 | async-start | bytes 4456448 | tf_op jit(solution)/shard_map/all_gather | solution.py:21
  8.0 218.0 %all-gather.7.cloned.1.call-start = ((), (), s32[]{:S(2)}) async-start(), calls=%async_computation.3 | async-start | bytes 8912896 | tf_op jit(solution)/shard_map/all_gather | solution.py:16
  8.7 335.1 %all-gather.11.cloned.1.call-start = ((), (), s32[]{:S(2)}) async-start(), calls=%async_computation.6 | async-start | bytes 15597568 | tf_op jit(solution)/shard_map/all_gather | solution.py:26
  9.3 409.5 %reduce-scatter.3.cloned.1.call-start = ((), (), s32[]{:S(2)}) async-start(), calls=%async_computation.5 | async-start | bytes 2228224 | tf_op jit(solution)/shard_map/reduce_scatter | solution.py:30
  234.5 118.0 %copy-start.1 = (s32[1,5]{1,0:T(1,128)S(1)}, s32[1,5]{1,0:T(1,128)}, u32[]{:S(2)}) copy-start(s32[1,5]{1,0:T(1,128)} %param.11) | copy-start | bytes 64
  234.5 257.1 %reduce-scatter.5.cloned.1.call-start = ((), (), s32[]{:S(2)}) async-start(), calls=%async_computation.7 | async-start | bytes 2228224 | tf_op jit(solution)/shard_map/reduce_scatter | solution.py:31
Sparse Core Ops, SparseCore 0:
  9.2 73.4 all-gather.4
  85.2 61.5 all-gather.8
  149.4 76.5 all-gather.6
  228.4 115.4 all-gather.10
  346.2 72.5 reduce-scatter.2
  421.2 70.3 reduce-scatter.4
where the time goes:
time: 501 us; the launch traced here: 500 us
  waiting for transfers between devices  468 us (93%)
  matrix products  17.8 us (4%)
  between operations  13.5 us (3%)
    all_gather x1, waiting for transfers between devices, on_device(): lax.all_gather(right_factors, 'dp', axis=1, tiled=True)  109 us
    all_gather x1, waiting for transfers between devices, on_device(): lax.all_gather(basis, 'dp', axis=0, tiled=True)  79.3 us
    all_gather x1, waiting for transfers between devices, on_device(): grads_full = lax.all_gather(out_grads, 'mp', axis=1, tiled=True)  73.3 us
    reduce_scatter x1, waiting for transfers between devices, on_device(): lax.psum_scatter(right_part, 'mp', scatter_dimension=1, tiled=True)  72.8 us
    reduce_scatter x1, waiting for transfers between devices, on_device(): lax.psum_scatter(left_part, 'mp', scatter_dimension=1, tiled=True)  66.2 us
    all_gather x1, waiting for transfers between devices, on_device(): lax.all_gather(left_factors, 'dp', axis=1, tiled=True)  64.1 us
  transfers between devices with their start and end apart: 6, of which 6 were waited for; matrix products, arithmetic and copies ran while one was open for 3% of the time, Pallas kernels for 0%

commit v1 on v0

v1 whole, which is shorter than its diff:
```python
import functools

import jax
import jax.numpy as jnp
from jax import lax
from jax.experimental import pallas as pl
from jax.experimental.pallas import tpu as pltpu
from jax.sharding import PartitionSpec as P

RANK = 32
TOK_DEV = 128
SEQ_DEV = 4
MESH = pl.DeviceIdType.MESH
BF16, F32 = jnp.bfloat16, jnp.float32

NX, NZ, NM = 4, 8, 16
T, O, E, C, I = 128, 512, 512, 256, 1792


def kernel(g_in, b_in, l_in, r_in, a_in, sp, out, gbuf, bbuf, lbuf, rbuf, abuf, prot, rprot, xrot, pbuf, pown, rsbuf, rfull,
           left, ends, sbuf, srecv, fin_s, fin_r, loc, ss, rs):
    d, m = lax.axis_index("dp"), lax.axis_index("mp")
    x, yh, c = d // 4, (d // 2) % 2, d % 2
    yl, z = m // NZ, m % NZ

    def dev(x_=None, yh_=None, c_=None, yl_=None, z_=None):
        pick = lambda new, old: old if new is None else new
        return (4 * pick(x_, x) + 2 * pick(yh_, yh) + pick(c_, c), NZ * pick(yl_, yl) + pick(z_, z))

    xs = [(x + k) % NX for k in range(NX)]
    zr, zl = (z + 1) % NZ, (z + NZ - 1) % NZ
    sibling, across, beside = dev(c_=1 - c), dev(yh_=1 - yh), dev(yl_=1 - yl)
    bit = (m // 2) % 2
    swap_m = m + 2 - 4 * bit
    swapped = (4 * x + 2 * (1 - yh) + c, swap_m)
    turn = (4 * (m // 4) + 2 * yh + c, 4 * x + m % 4)
    turns = x != m // 4

    def greet(to):
        pl.semaphore_signal(pltpu.get_barrier_semaphore(), inc=1, device_id=to, device_id_type=MESH)

    for k in (1, 2, 3):
        greet(dev(x_=xs[k]))
    for to in (sibling, across, swapped):
        greet(to)

    @pl.loop(1, NM)
    def _(k):
        greet((d, (m + k) % NM))

    pl.when(turns)(lambda: greet(turn))
    pl.semaphore_wait(pltpu.get_barrier_semaphore(), jnp.where(turns, 22, 21))

    used = [0]

    def take(n=1):
        used[0] += n
        return used[0] - n

    sent = []

    def copy(src, dst, to, sem, sem_there=None):
        sem_there = sem if sem_there is None else sem_there
        return pltpu.make_async_remote_copy(
            src_ref=src, dst_ref=dst, send_sem=ss.at[sem], recv_sem=rs.at[sem_there], device_id=to, device_id_type=MESH
        )

    def send(src, dst, to, sem):
        cp = copy(src, dst, to, sem)
        cp.start()
        sent.append(cp)

    def arrived(dst, sem):
        copy(dst, dst, sibling, sem).wait_recv()

    def gslot(mm, lo=0, n=T):
        return gbuf.at[(mm // 4) * 2 + mm % 2, pl.ds(((mm // 2) % 2) * T + lo, n)]

    def fslot(mm, lo=0, n=T):
        return rfull.at[mm, pl.ds(lo, n)]

    def arow(xx, lo=0, n=T):
        return abuf.at[pl.ds(xx * T + lo, n)]

    def bslot(xx, cc, lo=0, n=O):
        return bbuf.at[xx * 2 + cc, pl.ds(lo, n)]

    def spread(slot):
        sem_pair, sem = take(), take(16)
        half = T // 2

        def at(stream, direction, step):
            return sem + stream * 8 + direction * 4 + step

        def stage(stream, step):
            row = yl if stream == 0 else 1 - yl
            for direction, (to, sign) in enumerate(((zr, -1), (zl, 1))):
                origin = row * NZ + (z + sign * step + NZ) % NZ
                lo, n = (0, T) if step < 3 else (half * direction, half)
                send(slot(origin, lo, n), slot(origin, lo, n), dev(z_=to), at(stream, direction, step))

        def landed(stream, step):
            row = yl if stream == 0 else 1 - yl
            for direction, sign in ((0, -1), (1, 1)):
                origin = row * NZ + (z + sign * (step + 1) + NZ) % NZ
                lo, n = (0, T) if step < 3 else (half * direction, half)
                arrived(slot(origin, lo, n), at(stream, direction, step))

        def begin():
            send(slot(m), slot(m), beside, sem_pair)
            stage(0, 0)

        def second():
            arrived(slot((1 - yl) * NZ + z), sem_pair)
            stage(1, 0)

        def step(k):
            for stream in (0, 1):
                landed(stream, k)
                if k < 3:
                    stage(stream, k + 1)

        return begin, second, step

    places = [(a_in, arow(x)), (b_in, bslot(x, c)), (l_in, lbuf.at[yh * 2 + c]), (r_in, rbuf.at[yh * 2 + c])]
    own = [pltpu.make_async_copy(src, dst, loc.at[i]) for i, (src, dst) in enumerate(places)]
    own_g = pltpu.make_async_copy(g_in, gslot(m), loc.at[4])
    sem_g = take()
    move_g = copy(g_in, gslot(swap_m), swapped, sem_g)
    moves = yh != bit
    pl.when(moves)(lambda: move_g.start())
    pl.when(jnp.logical_not(moves))(lambda: own_g.start())

    def ring(src, slot, size):
        sem = take(4)
        half = size // 2

        def begin():
            send(src, slot(x, 0, size), dev(x_=xs[1]), sem)
            send(src, slot(x, 0, size), dev(x_=xs[3]), sem + 1)

        def first():
            arrived(slot(xs[3], 0, size), sem)
            send(slot(xs[3], 0, half), slot(xs[3], 0, half), dev(x_=xs[1]), sem + 2)
            arrived(slot(xs[1], 0, size), sem + 1)
            send(slot(xs[1], half, half), slot(xs[1], half, half), dev(x_=xs[3]), sem + 3)

        def last():
            arrived(slot(xs[2], 0, half), sem + 2)
            arrived(slot(xs[2], half, half), sem + 3)

        return begin, first, last

    a_begin, a_first, a_last = ring(a_in, arow, T)
    b_begin, b_first, b_last = ring(b_in, lambda xx, lo, n: bslot(xx, c, lo, n), O)
    a_begin()
    sem_r, sem_l, sem_rd, sem_ld, sem_bd = take(), take(), take(2), take(2), take(4)
    mine, other = yh * 2 + c, (1 - yh) * 2 + c
    send(r_in, rbuf.at[mine], across, sem_r)
    send(r_in, rbuf.at[mine], sibling, sem_rd)
    send(b_in, bslot(x, c), sibling, sem_bd)
    send(l_in, lbuf.at[mine], sibling, sem_ld)
    for cp in own:
        cp.start()

    row = lax.broadcasted_iota(jnp.int32, (8, 128), 0)
    tile = jnp.zeros((8, 128), jnp.int32)
    end = 0
    for k in range(SEQ_DEV):
        end = end + sp[0, k]
        tile = jnp.where(row == k, end, tile)
    ends[x] = tile
    sem_e = take(3)
    for k in (1, 2, 3):
        send(ends.at[x], ends.at[x], dev(x_=xs[k]), sem_e + k - 1)

    pl.when(moves)(lambda: copy(g_in, gslot(m), swapped, sem_g).wait_recv())
    pl.when(jnp.logical_not(moves))(lambda: own_g.wait())
    g_begin, g_second, g_step = spread(gslot)
    g_begin()
    g_second()
    g_step(0)
    a_first()
    b_begin()
    g_step(1)

    sem_rs = take(NM)
    f_begin, f_second, f_step = spread(fslot)

    def right(b):
        part = jnp.dot(abuf[...], rbuf[b], preferred_element_type=F32)
        for a in range(NX):
            block = part[a * T:(a + 1) * T]
            to = 4 * a + b
            pbuf[to] = block.astype(BF16)

            @pl.when(to == m)
            def _():
                pown[...] = block

            @pl.when(to != m)
            def _():
                copy(pbuf.at[to], rsbuf.at[m], (d, to), sem_rs + to, sem_rs + m).start()

    rsbuf[m] = jnp.zeros((T, C), BF16)
    a_last()
    own[0].wait()
    own[3].wait()
    right(mine)
    arrived(rbuf.at[yh * 2 + 1 - c], sem_rd)
    right(yh * 2 + 1 - c)
    g_step(2)
    b_first()
    send(bslot(xs[3], c), bslot(xs[3], c), sibling, sem_bd + 1)
    send(bslot(xs[1], c), bslot(xs[1], c), sibling, sem_bd + 2)
    arrived(rbuf.at[other], sem_r)
    send(rbuf.at[other], rbuf.at[other], sibling, sem_rd + 1)
    send(l_in, lbuf.at[mine], across, sem_l)
    right(other)
    arrived(rbuf.at[(1 - yh) * 2 + 1 - c], sem_rd + 1)
    right((1 - yh) * 2 + 1 - c)

    g_step(3)
    b_last()
    send(bslot(xs[2], c), bslot(xs[2], c), sibling, sem_bd + 3)
    own[1].wait()
    for k, xx in enumerate((x, xs[3], xs[1], xs[2])):
        arrived(bslot(xx, 1 - c), sem_bd + k)
    total = jnp.zeros((2 * T, E), F32)
    for j in range(8):
        total = total + jnp.dot(gbuf[j], bbuf[j], preferred_element_type=F32)
    prot[...] = total
    sem_rot, sem_xr = take(), take(3)
    send(prot.at[pl.ds((1 - yh) * T, T)], rprot, across, sem_rot)
    arrived(rprot, sem_rot)
    xrot[pl.ds(x * T, T)] = (prot[pl.ds(yh * T, T)] + rprot[...]).astype(BF16)
    for k in (1, 2, 3):
        send(xrot.at[pl.ds(x * T, T)], xrot.at[pl.ds(x * T, T)], dev(x_=xs[k]), sem_xr + k - 1)

    for src in range(NM):
        pl.when(src != m)(functools.partial(arrived, rsbuf.at[src], sem_rs + src))
    summed = pown[...]
    for src in range(NM):
        summed = summed + rsbuf[src].astype(F32)
    rfull[m] = summed.astype(BF16)
    f_begin()
    f_second()
    f_step(0)

    own[2].wait()
    arrived(lbuf.at[yh * 2 + 1 - c], sem_ld)
    arrived(lbuf.at[other], sem_l)
    send(lbuf.at[other], lbuf.at[other], sibling, sem_ld + 1)
    arrived(lbuf.at[(1 - yh) * 2 + 1 - c], sem_ld + 1)
    for k in (1, 2, 3):
        arrived(xrot.at[pl.ds(xs[4 - k] * T, T)], sem_xr + k - 1)
        arrived(ends.at[xs[4 - k]], sem_e + k - 1)
    f_step(1)
    for b in range(4):
        left[:, b * C:(b + 1) * C] = jnp.dot(xrot[...], lbuf[b], preferred_element_type=F32)
    f_step(2)
    f_step(3)

    slot = lax.broadcasted_iota(jnp.int32, (T, C), 0)
    for a in range(NX):
        stops = [jnp.broadcast_to(ends[a][k:k + 1, :1], (T, C)) for k in range(SEQ_DEV)]
        inside = [(slot < stops[0]) if k == 0 else (slot >= stops[k - 1]) & (slot < stops[k]) for k in range(SEQ_DEV)]
        for b in range(4):
            prod = left[a * T:(a + 1) * T, b * C:(b + 1) * C] * rfull[4 * a + b].astype(F32)
            rows = [jnp.sum(jnp.where(one, prod, 0.0), axis=0, keepdims=True) for one in inside]
            sbuf[4 * a + b] = jnp.concatenate(rows + [jnp.zeros((8 - SEQ_DEV, C), F32)], axis=0)

    sem_s, sem_f = take(NM), take()
    for to in range(NM):
        @pl.when(to != m)
        def _():
            copy(sbuf.at[to], srecv.at[m], (d, to), sem_s + to, sem_s + m).start()
    srecv[m] = sbuf[m]
    for src in range(NM):
        pl.when(src != m)(functools.partial(arrived, srecv.at[src], sem_s + src))
    scores = srecv[0]
    for src in range(1, NM):
        scores = scores + srecv[src]
    column, query = (lax.broadcasted_iota(jnp.int32, (C, 128), k) for k in (0, 1))
    ranks = (column // RANK == query).astype(F32)
    scale = 1.0 / jnp.sqrt(jnp.float32(RANK * TOK_DEV))
    fin_s[...] = jnp.dot(scores, ranks, precision=lax.Precision.HIGHEST, preferred_element_type=F32) * scale
    last = copy(fin_s, fin_r, turn, sem_f)

    @pl.when(turns)
    def _():
        last.start()
        last.wait()

    @pl.when(jnp.logical_not(turns))
    def _():
        fin_r[...] = fin_s[...]

    out[...] = fin_r[:SEQ_DEV, :C // RANK]

    for cp in sent:
        cp.wait_send()
    pl.when(moves)(lambda: move_g.wait_send())
    for to in range(NM):
        @pl.when(to != m)
        def _():
            copy(pbuf.at[to], rsbuf.at[m], (d, to), sem_rs + to, sem_rs + m).wait_send()
            copy(sbuf.at[to], srecv.at[m], (d, to), sem_s + to, sem_s + m).wait_send()
    assert used[0] <= NSEM, used[0]


NSEM = 128


def on_device(out_grads, basis, left_factors, right_factors, activations, spans):
    vmem = pltpu.VMEM
    return pl.pallas_call(
        kernel,
        out_shape=jax.ShapeDtypeStruct((SEQ_DEV, C // RANK), F32),
        in_specs=[pl.BlockSpec(memory_space=pl.ANY)] * 5 + [pl.BlockSpec(memory_space=pltpu.SMEM)],
        out_specs=pl.BlockSpec(memory_space=vmem),
        scratch_shapes=[
            vmem((8, 2 * T, O), BF16),
            vmem((8, O, E), BF16),
            vmem((4, E, C), BF16),
            vmem((4, I, C), BF16),
            vmem((NX * T, I), BF16),
            vmem((2 * T, E), F32),
            vmem((T, E), F32),
            vmem((NX * T, E), BF16),
            vmem((NM, T, C), BF16),
            vmem((T, C), F32),
            vmem((NM, T, C), BF16),
            vmem((NM, T, C), BF16),
            vmem((NX * T, 4 * C), F32),
            vmem((NX, 8, 128), jnp.int32),
            vmem((NM, 8, C), F32),
            vmem((NM, 8, C), F32),
            vmem((8, 128), F32),
            vmem((8, 128), F32),
            pltpu.SemaphoreType.DMA((5,)),
            pltpu.SemaphoreType.DMA((NSEM,)),
            pltpu.SemaphoreType.DMA((NSEM,)),
        ],
        compiler_params=pltpu.CompilerParams(collective_id=0, has_side_effects=True, vmem_limit_bytes=48 << 20),
    )(out_grads, basis, left_factors, right_factors, activations, spans)


def solution(mesh):
    placed = (
        P("dp", "mp"),
        P("dp", "mp"),
        P("mp", "dp"),
        P("mp", "dp"),
        P("dp", "mp"),
        P("dp", None),
    )
    return jax.shard_map(
        on_device, mesh=mesh, in_specs=placed, out_specs=P("dp", "mp"), check_vma=False
    )
```

time: 501 us -> 129 us (0.26)
  the two profiles are of different devices: /device:TPU:8 before, /device:TPU:6 now
where the time goes in v1:
time: 129 us
  Pallas kernels  123 us (95%)
  local copies, waits for them, and re-layouts  6.33 us (5%)
    pallas_call x1, Pallas kernels, on_device(): pl.pallas_call(kernel, out_shape=jax.ShapeDtypeStruct((SEQ_DEV, C // RANK...  123 us
    unnamed x13, local copies, waits for them, and re-layouts  6.33 us

profile of v1, /device:TPU:6, one launch (start us, length us, event | category | flops | bytes accessed | tf_op | source)
XLA Modules:
  0.0 129.2 jit_solution(9988111536584180430)
XLA Ops:
  0.0 0.0 copy-start
  0.0 1.2 copy-done
  1.2 0.0 copy-start.1
  1.2 1.0 copy-done.1
  2.2 0.0 copy-start.2
  2.2 1.0 copy-done.2
  3.2 0.0 copy-start.3
  3.2 0.9 copy-done.3
  4.2 0.0 copy-start.4
  4.2 0.9 copy-done.4
  5.1 0.0 copy-start.5
  5.1 0.7 copy-done.5
  5.8 122.8 %shard_map.64 = f32[4,8]{1,0:T(4,128)S(1)} custom-call(bf16[128,512]{1,0:T(8,128)(2,1)S(1)} %copy-done.4, bf16[512,512]{1,0:T(8,128)(2,1)S(1)} %copy-done.1, bf16[512,256]{1,0:T(8,128)(2,1)S(1)} %copy-done.3, bf16[1792,256]{1,0:T(8,128)(2,1)S(1)} %copy-done, bf16[128,1792]{1,0:T(8,128)(2,1)S(1)} %copy-done.2, s32[1,5]{1,0:T(1,128)S(1)} %copy-done.5), custom_call_target="tpu_custom_call" | custom-call | tf_op jit(solution)/shard_map/pallas_call | solution.py:317
  128.6 0.6 copy.8
Async XLA Ops:
  0.0 1.2 copy-start
  1.2 1.0 copy-start.1
  2.2 1.0 copy-start.2
  3.2 0.9 copy-start.3
  4.2 0.9 copy-start.4
  5.1 0.7 copy-start.5

commit v2 on v1

v2 whole, which is shorter than its diff:
```python
import functools

import jax
import jax.numpy as jnp
from jax import lax
from jax.experimental import pallas as pl
from jax.experimental.pallas import tpu as pltpu
from jax.sharding import PartitionSpec as P

RANK = 32
TOK_DEV = 128
SEQ_DEV = 4
MESH = pl.DeviceIdType.MESH
BF16, F32 = jnp.bfloat16, jnp.float32

NX, NZ, NM = 4, 8, 16
T, O, E, C, I = 128, 512, 512, 256, 1792


def kernel(g_in, b_in, l_in, r_in, a_in, sp, out, gbuf, bbuf, lbuf, rbuf, abuf, prot, rprot, xrot, pf, pb, yb, zsend, zrecv,
           rfull, left, ends, sbuf, ssend, srecv, fin_s, fin_r, loc, ss, rs):
    d, m = lax.axis_index("dp"), lax.axis_index("mp")
    x, yh, c = d // 4, (d // 2) % 2, d % 2
    yl, z = m // NZ, m % NZ

    def dev(x_=None, yh_=None, c_=None, yl_=None, z_=None):
        pick = lambda new, old: old if new is None else new
        return (4 * pick(x_, x) + 2 * pick(yh_, yh) + pick(c_, c), NZ * pick(yl_, yl) + pick(z_, z))

    xs = [(x + k) % NX for k in range(NX)]
    zr, zl = (z + 1) % NZ, (z + NZ - 1) % NZ
    sibling, across, beside = dev(c_=1 - c), dev(yh_=1 - yh), dev(yl_=1 - yl)
    bit = (m // 2) % 2
    swap_m = m + 2 - 4 * bit
    swapped = (4 * x + 2 * (1 - yh) + c, swap_m)
    turn = (4 * (m // 4) + 2 * yh + c, 4 * x + m % 4)
    turns = x != m // 4

    def greet(to):
        pl.semaphore_signal(pltpu.get_barrier_semaphore(), inc=1, device_id=to, device_id_type=MESH)

    near = [dev(x_=xs[k]) for k in (1, 2, 3)] + [dev(z_=zr), dev(z_=zl), sibling, across, beside, swapped]
    for to in near:
        greet(to)
    pl.semaphore_wait(pltpu.get_barrier_semaphore(), len(near))

    used = [0]

    def take(n=1):
        used[0] += n
        return used[0] - n

    sent = []

    def copy(src, dst, to, sem, sem_there=None):
        sem_there = sem if sem_there is None else sem_there
        return pltpu.make_async_remote_copy(
            src_ref=src, dst_ref=dst, send_sem=ss.at[sem], recv_sem=rs.at[sem_there], device_id=to, device_id_type=MESH
        )

    def send(src, dst, to, sem):
        cp = copy(src, dst, to, sem)
        cp.start()
        sent.append(cp)

    def arrived(dst, sem):
        copy(dst, dst, sibling, sem).wait_recv()

    def gslot(mm, lo=0, n=T):
        return gbuf.at[(mm // 4) * 2 + mm % 2, pl.ds(((mm // 2) % 2) * T + lo, n)]

    def fslot(mm, lo=0, n=T):
        return rfull.at[mm, pl.ds(lo, n)]

    def arow(xx, lo=0, n=T):
        return abuf.at[pl.ds(xx * T + lo, n)]

    def bslot(xx, cc, lo=0, n=O):
        return bbuf.at[xx * 2 + cc, pl.ds(lo, n)]

    def spread(slot):
        sem_pair, sem = take(), take(16)
        half = T // 2

        def at(stream, direction, step):
            return sem + stream * 8 + direction * 4 + step

        def stage(stream, step):
            row = yl if stream == 0 else 1 - yl
            for direction, (to, sign) in enumerate(((zr, -1), (zl, 1))):
                origin = row * NZ + (z + sign * step + NZ) % NZ
                lo, n = (0, T) if step < 3 else (half * direction, half)
                send(slot(origin, lo, n), slot(origin, lo, n), dev(z_=to), at(stream, direction, step))

        def landed(stream, step):
            row = yl if stream == 0 else 1 - yl
            for direction, sign in ((0, -1), (1, 1)):
                origin = row * NZ + (z + sign * (step + 1) + NZ) % NZ
                lo, n = (0, T) if step < 3 else (half * direction, half)
                arrived(slot(origin, lo, n), at(stream, direction, step))

        def begin():
            send(slot(m), slot(m), beside, sem_pair)
            stage(0, 0)

        def second():
            arrived(slot((1 - yl) * NZ + z), sem_pair)
            stage(1, 0)

        def go(stream, k):
            landed(stream, k)
            if k < 3:
                stage(stream, k + 1)

        return begin, second, go

    places = [(a_in, arow(x)), (b_in, bslot(x, c)), (l_in, lbuf.at[yh * 2 + c]), (r_in, rbuf.at[yh * 2 + c])]
    own = [pltpu.make_async_copy(src, dst, loc.at[i]) for i, (src, dst) in enumerate(places)]
    own_g = pltpu.make_async_copy(g_in, gslot(m), loc.at[4])
    sem_g = take()
    move_g = copy(g_in, gslot(swap_m), swapped, sem_g)
    moves = yh != bit
    pl.when(moves)(lambda: move_g.start())
    pl.when(jnp.logical_not(moves))(lambda: own_g.start())

    def ring(src, slot, size, cuts):
        sem = take(2 * len(cuts))
        half = size // 2
        pieces = [(lo, hi - lo) for lo, hi in zip(cuts, cuts[1:])]

        def begin(k):
            lo, n = pieces[k]
            for way, to in ((0, xs[1]), (1, xs[3])):
                send(src.at[pl.ds(lo, n)], slot(x, lo, n), dev(x_=to), sem + 2 * k + way)

        def first():
            for way, to, came in ((0, xs[1], xs[3]), (1, xs[3], xs[1])):
                for k, (lo, n) in enumerate(pieces):
                    arrived(slot(came, lo, n), sem + 2 * k + way)
                send(slot(came, way * half, half), slot(came, way * half, half), dev(x_=to), sem + 2 * len(pieces) + way)

        def last():
            for way in range(2):
                arrived(slot(xs[2], way * half, half), sem + 2 * len(pieces) + way)

        return begin, first, last

    a_begin, a_first, a_last = ring(a_in, arow, T, (0, T))
    b_begin, b_first, b_last = ring(b_in, lambda xx, lo, n: bslot(xx, c, lo, n), O, (0, O // 4, O))
    sem_l, sem_rd, sem_ld, sem_bd = take(), take(2), take(2), take(4)
    sem_r = take(2)
    r_cut = I // 4
    mine, other = yh * 2 + c, (1 - yh) * 2 + c

    def r_rows(slot, k):
        return slot.at[pl.ds(k * r_cut, r_cut + k * (I - 2 * r_cut))]

    def r_send(k):
        send(r_rows(r_in, k), r_rows(rbuf.at[mine], k), across, sem_r + k)

    row = lax.broadcasted_iota(jnp.int32, (8, 128), 0)
    tile = jnp.zeros((8, 128), jnp.int32)
    end = 0
    for k in range(SEQ_DEV):
        end = end + sp[0, k]
        tile = jnp.where(row == k, end, tile)
    ends[x] = tile
    sem_e = take(3)
    for k in (1, 2, 3):
        send(ends.at[x], ends.at[x], dev(x_=xs[k]), sem_e + k - 1)
    a_begin(0)
    b_begin(0)
    r_send(0)
    send(r_in, rbuf.at[mine], sibling, sem_rd)
    send(b_in, bslot(x, c), sibling, sem_bd)
    send(l_in, lbuf.at[mine], sibling, sem_ld)
    for cp in own:
        cp.start()

    pl.when(moves)(lambda: copy(g_in, gslot(m), swapped, sem_g).wait_recv())
    pl.when(jnp.logical_not(moves))(lambda: own_g.wait())
    g_begin, g_second, g_go = spread(gslot)
    g_begin()
    r_send(1)
    g_second()
    g_go(0, 0)
    a_first()
    b_begin(1)
    g_go(1, 0)
    g_go(0, 1)

    def right(b):
        part = jnp.dot(abuf[...], rbuf[b], preferred_element_type=F32)
        for a in range(NX):
            pf[4 * a + b] = part[a * T:(a + 1) * T]

    sem_y = take(NZ)

    def pair_sum(b):
        for zz in (b, b + 4):
            pb[zz] = pf[(1 - yl) * NZ + zz].astype(BF16)
            send(pb.at[zz], yb.at[zz], beside, sem_y + zz)

    a_last()
    own[0].wait()
    own[3].wait()
    g_go(1, 1)
    right(mine)
    arrived(rbuf.at[yh * 2 + 1 - c], sem_rd)
    g_go(0, 2)
    right(yh * 2 + 1 - c)
    g_go(1, 2)
    pair_sum(mine)
    pair_sum(yh * 2 + 1 - c)
    for k in range(2):
        arrived(r_rows(rbuf.at[other], k), sem_r + k)
    send(rbuf.at[other], rbuf.at[other], sibling, sem_rd + 1)
    right(other)
    pair_sum(other)
    b_first()
    send(bslot(xs[3], c), bslot(xs[3], c), sibling, sem_bd + 1)
    send(bslot(xs[1], c), bslot(xs[1], c), sibling, sem_bd + 2)
    arrived(rbuf.at[(1 - yh) * 2 + 1 - c], sem_rd + 1)
    right((1 - yh) * 2 + 1 - c)
    pair_sum((1 - yh) * 2 + 1 - c)
    send(l_in, lbuf.at[mine], across, sem_l)
    g_go(0, 3)
    g_go(1, 3)

    zs = [(z + k) % NZ for k in (4, 3, 5, 2, 6, 1, 7, 0)]

    def both(k):
        arrived(yb.at[zs[k]], sem_y + zs[k])

    def partial(k, u):
        cols = pl.ds(u * (C // 2), C // 2)
        return pf[yl * NZ + zs[k], :, cols] + yb[zs[k], :, cols].astype(F32)

    sem_z = take(16)
    half = T // 2

    def hop(way, step, u):
        return sem_z + way * 8 + step * 2 + u

    def z_first():
        both(0)
        for u in range(2):
            chunk = partial(0, u)
            for way, to in enumerate((zr, zl)):
                zsend[way, 0, u, :half] = chunk[way * half:(way + 1) * half]
                send(zsend.at[way, 0, u, pl.ds(0, half)], zrecv.at[way, 0, u, pl.ds(0, half)], dev(z_=to), hop(way, 0, u))

    def z_next(step):
        for way in range(2):
            both(2 * step - 1 + way)
        for u in range(2):
            for way, to in enumerate((zr, zl)):
                n = half if step == 1 else T
                arrived(zrecv.at[way, step - 1, u, pl.ds(0, n)], hop(way, step - 1, u))
                chunk = partial(2 * step - 1 + way, u)
                if step == 1:
                    zsend[way, step, u] = chunk
                    rows = pl.ds(way * half, half)
                    zsend[way, step, u, rows] = zsend[way, step, u, rows] + zrecv[way, 0, u, :half]
                else:
                    zsend[way, step, u] = chunk + zrecv[way, step - 1, u]
                send(zsend.at[way, step, u], zrecv.at[way, step, u], dev(z_=to), hop(way, step, u))

    z_first()
    b_last()
    send(bslot(xs[2], c), bslot(xs[2], c), sibling, sem_bd + 3)
    z_next(1)

    own[1].wait()
    for k, xx in enumerate((x, xs[3], xs[1], xs[2])):
        arrived(bslot(xx, 1 - c), sem_bd + k)
    total = jnp.zeros((2 * T, E), F32)
    for j in range(8):
        total = total + jnp.dot(gbuf[j], bbuf[j], preferred_element_type=F32)
    prot[...] = total
    sem_rot, sem_xr = take(), take(3)
    send(prot.at[pl.ds((1 - yh) * T, T)], rprot, across, sem_rot)
    z_next(2)
    z_next(3)
    arrived(rprot, sem_rot)
    xrot[pl.ds(x * T, T)] = (prot[pl.ds(yh * T, T)] + rprot[...]).astype(BF16)
    for k in (1, 2, 3):
        send(xrot.at[pl.ds(x * T, T)], xrot.at[pl.ds(x * T, T)], dev(x_=xs[k]), sem_xr + k - 1)

    slot = lax.broadcasted_iota(jnp.int32, (T, C), 0)

    def product(mm):
        prod = left[mm] * rfull[mm].astype(F32)
        stops = ends[mm // 4]
        below = [slot < jnp.broadcast_to(stops[k:k + 1, :1], (T, C)) for k in range(SEQ_DEV)]
        rows = []
        for k in range(SEQ_DEV):
            inside = below[0] if k == 0 else below[k] & jnp.logical_not(below[k - 1])
            rows.append(jnp.sum(jnp.where(inside, prod, 0.0), axis=0, keepdims=True))
        sbuf[pl.ds(pl.multiple_of(mm * 8, 8), 8)] = jnp.concatenate(rows + [jnp.zeros((8 - SEQ_DEV, C), F32)], axis=0)

    both(7)
    for u in range(2):
        total = partial(7, u)
        for way in range(2):
            arrived(zrecv.at[way, 3, u], hop(way, 3, u))
            total = total + zrecv[way, 3, u]
        rfull[m, :, u * (C // 2):(u + 1) * (C // 2)] = total.astype(BF16)
    f_begin, f_second, f_go = spread(fslot)
    f_begin()
    f_second()
    f_go(0, 0)
    f_go(1, 0)
    own[2].wait()
    arrived(lbuf.at[yh * 2 + 1 - c], sem_ld)
    arrived(lbuf.at[other], sem_l)
    send(lbuf.at[other], lbuf.at[other], sibling, sem_ld + 1)
    arrived(lbuf.at[(1 - yh) * 2 + 1 - c], sem_ld + 1)
    for k in (1, 2, 3):
        arrived(xrot.at[pl.ds(xs[4 - k] * T, T)], sem_xr + k - 1)
        arrived(ends.at[xs[4 - k]], sem_e + k - 1)
    for b in range(4):
        part = jnp.dot(xrot[...], lbuf[b], preferred_element_type=F32)
        for a in range(NX):
            left[4 * a + b] = part[a * T:(a + 1) * T]
    f_go(0, 1)
    f_go(1, 1)
    product(m)
    product((1 - yl) * NZ + z)
    for k in range(4):
        for stream in range(2):
            if k >= 2:
                f_go(stream, k)
            for far in ((k + 1, NZ - 1 - k) if k < 3 else (4,)):
                product((yl if stream == 0 else 1 - yl) * NZ + (z + far) % NZ)

    sem_s, sem_f = take(NM), take()
    column, query = (lax.broadcasted_iota(jnp.int32, (C, 128), k) for k in (0, 1))
    ranks = (column // RANK == query).astype(F32)
    tiles = jnp.dot(sbuf[...], ranks, precision=lax.Precision.HIGHEST, preferred_element_type=F32)
    for to in range(NM):
        ssend[to] = tiles[to * 8:(to + 1) * 8]

        @pl.when(to != m)
        def _():
            copy(ssend.at[to], srecv.at[m], (d, to), sem_s + to, sem_s + m).start()
    srecv[m] = ssend[m]
    for src in range(NM):
        pl.when(src != m)(functools.partial(arrived, srecv.at[src], sem_s + src))
    scores = srecv[0]
    for src in range(1, NM):
        scores = scores + srecv[src]
    fin_s[...] = scores * (1.0 / jnp.sqrt(jnp.float32(RANK * TOK_DEV)))
    last = copy(fin_s, fin_r, turn, sem_f)

    @pl.when(turns)
    def _():
        last.start()
        last.wait()

    @pl.when(jnp.logical_not(turns))
    def _():
        fin_r[...] = fin_s[...]

    out[...] = fin_r[:SEQ_DEV, :C // RANK]

    for cp in sent:
        cp.wait_send()
    pl.when(moves)(lambda: move_g.wait_send())
    for to in range(NM):
        @pl.when(to != m)
        def _():
            copy(ssend.at[to], srecv.at[m], (d, to), sem_s + to, sem_s + m).wait_send()
    assert used[0] <= NSEM, used[0]


NSEM = 160


def on_device(out_grads, basis, left_factors, right_factors, activations, spans):
    vmem = pltpu.VMEM
    return pl.pallas_call(
        kernel,
        out_shape=jax.ShapeDtypeStruct((SEQ_DEV, C // RANK), F32),
        in_specs=[pl.BlockSpec(memory_space=pltpu.HBM)] * 5 + [pl.BlockSpec(memory_space=pltpu.SMEM)],
        out_specs=pl.BlockSpec(memory_space=vmem),
        scratch_shapes=[
            vmem((8, 2 * T, O), BF16),
            vmem((8, O, E), BF16),
            vmem((4, E, C), BF16),
            vmem((4, I, C), BF16),
            vmem((NX * T, I), BF16),
            vmem((2 * T, E), F32),
            vmem((T, E), F32),
            vmem((NX * T, E), BF16),
            vmem((NM, T, C), F32),
            vmem((NZ, T, C), BF16),
            vmem((NZ, T, C), BF16),
            vmem((2, 4, 2, T, C // 2), F32),
            vmem((2, 4, 2, T, C // 2), F32),
            vmem((NM, T, C), BF16),
            vmem((NM, T, C), F32),
            vmem((NX, 8, 128), jnp.int32),
            vmem((NM * 8, C), F32),
            vmem((NM, 8, 128), F32),
            vmem((NM, 8, 128), F32),
            vmem((8, 128), F32),
            vmem((8, 128), F32),
            pltpu.SemaphoreType.DMA((5,)),
            pltpu.SemaphoreType.DMA((NSEM,)),
            pltpu.SemaphoreType.DMA((NSEM,)),
        ],
        compiler_params=pltpu.CompilerParams(collective_id=0, has_side_effects=True, vmem_limit_bytes=60 << 20),
    )(out_grads, basis, left_factors, right_factors, activations, spans)


def solution(mesh):
    placed = (
        P("dp", "mp"),
        P("dp", "mp"),
        P("mp", "dp"),
        P("mp", "dp"),
        P("dp", "mp"),
        P("dp", None),
    )
    return jax.shard_map(
        on_device, mesh=mesh, in_specs=placed, out_specs=P("dp", "mp"), check_vma=False
    )
```

time: 129 us -> 98.8 us (0.77)
  the two profiles are of different devices: /device:TPU:6 before, /device:TPU:8 now
where the time goes in v2:
time: 98.8 us; the launch traced here: 98 us
  Pallas kernels  96.8 us (98%)
  local copies, waits for them, and re-layouts  1.26 us (1%)
    pallas_call x1, Pallas kernels, on_device(): pl.pallas_call(kernel, out_shape=jax.ShapeDtypeStruct((SEQ_DEV, C // RANK...  96.8 us

profile of v2, /device:TPU:8, one launch (start us, length us, event | category | flops | bytes accessed | tf_op | source)
XLA Modules:
  0.0 98.0 jit_solution(8110295426909159021)
XLA Ops:
  0.0 96.8 %shard_map.64 = f32[4,8]{1,0:T(4,128)} custom-call(bf16[128,512]{1,0:T(8,128)(2,1)} %g_in.1, bf16[512,512]{1,0:T(8,128)(2,1)} %b_in.1, bf16[512,256]{1,0:T(8,128)(2,1)} %l_in.1, bf16[1792,256]{1,0:T(8,128)(2,1)} %r_in.1, bf16[128,1792]{1,0:T(8,128)(2,1)} %a_in.1, s32[1,5]{1,0:T(1,128)} %sp.1), custom_call_target="tpu_custom_call" | custom-call | tf_op jit(solution)/shard_map/pallas_call | solution.py:382
  96.8 1.3 %copy.8 = f32[4,8]{1,0:T(4,128)} copy(f32[4,8]{1,0:T(4,128)} %shard_map.64) | data formatting | bytes 256

commit v3 on v2

v3 whole, which is shorter than its diff:
```python
import functools

import jax
import jax.numpy as jnp
from jax import lax
from jax.experimental import pallas as pl
from jax.experimental.pallas import tpu as pltpu
from jax.sharding import PartitionSpec as P

RANK = 32
TOK_DEV = 128
SEQ_DEV = 4
MESH = pl.DeviceIdType.MESH
BF16, F32 = jnp.bfloat16, jnp.float32

NX, NZ, NM = 4, 8, 16
T, O, E, C, I = 128, 512, 512, 256, 1792
H = T // 2


def kernel(g_in, b_in, l_in, r_in, a_in, sp, out, gbuf, bbuf, lbuf, rbuf, abuf, prot, rprot, xrot, pf, pb, yb, zsend, zrecv,
           rfull, left, ends, sbuf, ssend, srecv, loc, ss, rs):
    d, m = lax.axis_index("dp"), lax.axis_index("mp")
    x, yh, c = d // 4, (d // 2) % 2, d % 2
    yl, z = m // NZ, m % NZ

    def dev(x_=None, yh_=None, c_=None, yl_=None, z_=None):
        pick = lambda new, old: old if new is None else new
        return (4 * pick(x_, x) + 2 * pick(yh_, yh) + pick(c_, c), NZ * pick(yl_, yl) + pick(z_, z))

    xs = [(x + k) % NX for k in range(NX)]
    zr, zl = (z + 1) % NZ, (z + NZ - 1) % NZ
    sibling, across, beside = dev(c_=1 - c), dev(yh_=1 - yh), dev(yl_=1 - yl)
    bit = (m // 2) % 2
    swap_m = m + 2 - 4 * bit
    swapped = (4 * x + 2 * (1 - yh) + c, swap_m)

    def greet(to):
        pl.semaphore_signal(pltpu.get_barrier_semaphore(), inc=1, device_id=to, device_id_type=MESH)

    near = [dev(x_=xs[k]) for k in (1, 2, 3)] + [dev(z_=zr), dev(z_=zl), sibling, across, beside, swapped]
    for to in near:
        greet(to)
    pl.semaphore_wait(pltpu.get_barrier_semaphore(), len(near))

    used = [0]

    def take(n=1):
        used[0] += n
        return used[0] - n

    sent = []

    def copy(src, dst, to, sem, sem_there=None):
        sem_there = sem if sem_there is None else sem_there
        return pltpu.make_async_remote_copy(
            src_ref=src, dst_ref=dst, send_sem=ss.at[sem], recv_sem=rs.at[sem_there], device_id=to, device_id_type=MESH
        )

    def send(src, dst, to, sem):
        cp = copy(src, dst, to, sem)
        cp.start()
        sent.append(cp)

    def arrived(dst, sem):
        copy(dst, dst, sibling, sem).wait_recv()

    def gslot(mm, lo=0, n=T):
        return gbuf.at[(mm // 4) * 2 + mm % 2, pl.ds(((mm // 2) % 2) * T + lo, n)]

    def fslot(u):
        return lambda mm, lo=0, n=H: rfull.at[u, mm % NZ, pl.ds((mm // NZ) * H + lo, n)]

    def arow(xx, lo=0, n=T):
        return abuf.at[pl.ds(xx * T + lo, n)]

    def bslot(xx, cc, lo=0, n=O):
        return bbuf.at[xx * 2 + cc, pl.ds(lo, n)]

    def spread(slot, rows):
        sem_pair, sem = take(), take(16)
        half = rows // 2

        def at(stream, direction, step):
            return sem + stream * 8 + direction * 4 + step

        def stage(stream, step):
            row = yl if stream == 0 else 1 - yl
            for direction, (to, sign) in enumerate(((zr, -1), (zl, 1))):
                origin = row * NZ + (z + sign * step + NZ) % NZ
                lo, n = (0, rows) if step < 3 else (half * direction, half)
                send(slot(origin, lo, n), slot(origin, lo, n), dev(z_=to), at(stream, direction, step))

        def landed(stream, step):
            row = yl if stream == 0 else 1 - yl
            for direction, sign in ((0, -1), (1, 1)):
                origin = row * NZ + (z + sign * (step + 1) + NZ) % NZ
                lo, n = (0, rows) if step < 3 else (half * direction, half)
                arrived(slot(origin, lo, n), at(stream, direction, step))

        def begin():
            send(slot(m), slot(m), beside, sem_pair)
            stage(0, 0)

        def second():
            arrived(slot((1 - yl) * NZ + z), sem_pair)
            stage(1, 0)

        def go(stream, k):
            landed(stream, k)
            if k < 3:
                stage(stream, k + 1)

        return begin, second, go

    def relay(slot, rows):
        sem, half = take(17), rows // 2

        def piece(row, direction, step):
            origin = row * NZ + (z + (-step, step)[direction] + NZ) % NZ
            return slot(origin, 0, rows) if step < 4 else slot(origin, half * direction, half)

        def begin():
            for direction, to in enumerate((zr, zl)):
                send(slot(m), slot(m), dev(z_=to), sem + direction)
            send(slot(m), slot(m), beside, sem + 16)

        def go(k):
            for direction, to in enumerate((zr, zl)):
                block = piece(yl, direction, k + 1)
                arrived(block, sem + 2 * k + direction)
                if k < 3:
                    onward = block if k < 2 else slot(yl * NZ + (z + (-3, 3)[direction] + NZ) % NZ, half * direction, half)
                    send(onward, onward, dev(z_=to), sem + 2 * (k + 1) + direction)
                send(block, block, beside, sem + 8 + 2 * k + direction)

        def pair(k):
            if k < 0:
                arrived(slot((1 - yl) * NZ + z), sem + 16)
            else:
                for direction in range(2):
                    arrived(piece(1 - yl, direction, k + 1), sem + 8 + 2 * k + direction)

        return begin, go, pair

    places = [(a_in, arow(x)), (b_in, bslot(x, c)), (l_in, lbuf.at[yh * 2 + c]), (r_in, rbuf.at[yh * 2 + c])]
    own = [pltpu.make_async_copy(src, dst, loc.at[i]) for i, (src, dst) in enumerate(places)]
    own_g = pltpu.make_async_copy(g_in, gslot(m), loc.at[4])
    sem_g = take()
    move_g = copy(g_in, gslot(swap_m), swapped, sem_g)
    moves = yh != bit
    pl.when(moves)(lambda: move_g.start())
    pl.when(jnp.logical_not(moves))(lambda: own_g.start())

    def ring(src, slot, size, cuts):
        sem = take(2 * len(cuts))
        half = size // 2
        pieces = [(lo, hi - lo) for lo, hi in zip(cuts, cuts[1:])]

        def begin(k):
            lo, n = pieces[k]
            for way, to in ((0, xs[1]), (1, xs[3])):
                send(src.at[pl.ds(lo, n)], slot(x, lo, n), dev(x_=to), sem + 2 * k + way)

        def first():
            for way, to, came in ((0, xs[1], xs[3]), (1, xs[3], xs[1])):
                for k, (lo, n) in enumerate(pieces):
                    arrived(slot(came, lo, n), sem + 2 * k + way)
                send(slot(came, way * half, half), slot(came, way * half, half), dev(x_=to), sem + 2 * len(pieces) + way)

        def last():
            for way in range(2):
                arrived(slot(xs[2], way * half, half), sem + 2 * len(pieces) + way)

        return begin, first, last

    a_begin, a_first, a_last = ring(a_in, arow, T, (0, T))
    b_begin, b_first, b_last = ring(b_in, lambda xx, lo, n: bslot(xx, c, lo, n), O, (0, O // 4, O))
    sem_l, sem_rd, sem_ld, sem_bd = take(), take(2), take(2), take(4)
    sem_r = take(2)
    r_cut = I // 4
    mine, other = yh * 2 + c, (1 - yh) * 2 + c

    def r_rows(slot, k):
        return slot.at[pl.ds(k * r_cut, r_cut + k * (I - 2 * r_cut))]

    def r_send(k):
        send(r_rows(r_in, k), r_rows(rbuf.at[mine], k), across, sem_r + k)

    row = lax.broadcasted_iota(jnp.int32, (8, 128), 0)
    tile = jnp.zeros((8, 128), jnp.int32)
    end = 0
    for k in range(SEQ_DEV):
        end = end + sp[0, k]
        tile = jnp.where(row == k, end, tile)
    ends[x] = tile
    sem_e = take(3)
    for k in (1, 2, 3):
        send(ends.at[x], ends.at[x], dev(x_=xs[k]), sem_e + k - 1)
    a_begin(0)
    b_begin(0)
    r_send(0)
    send(r_in, rbuf.at[mine], sibling, sem_rd)
    send(b_in, bslot(x, c), sibling, sem_bd)
    send(l_in, lbuf.at[mine], sibling, sem_ld)
    for cp in own:
        cp.start()

    pl.when(moves)(lambda: copy(g_in, gslot(m), swapped, sem_g).wait_recv())
    pl.when(jnp.logical_not(moves))(lambda: own_g.wait())
    g_begin, g_second, g_go = spread(gslot, T)
    g_begin()
    r_send(1)
    g_go(0, 0)
    g_second()
    a_first()
    b_begin(1)
    g_go(0, 1)
    g_go(1, 0)

    def right(u, cc):
        part = jnp.dot(abuf[...], rbuf[(mine // 2 if u == 0 else other // 2) * 2 + cc], preferred_element_type=F32)
        for a in range(NX):
            pf[u, 2 * a + cc] = part[a * T:(a + 1) * T]

    zs = [(z + k) % NZ for k in (4, 3, 5, 2, 6, 1, 7, 0)]
    sem_y, sem_z = take(4), take(16)
    quarter = H // 2
    keep, give = pl.ds(yl * H, H), pl.ds((1 - yl) * H, H)

    lots = ((0, 3), (3, 5))
    met = set()

    def pair_sum(u):
        for k, zz in enumerate(zs):
            pb[u, k] = pf[u, zz, give].astype(BF16)
            for lot, (first, n) in enumerate(lots):
                if k == first + n - 1:
                    blocks = pl.ds(first, n)
                    send(pb.at[u, blocks], yb.at[u, blocks], beside, sem_y + 2 * u + lot)

    def partial(u, k):
        lot = 0 if k < lots[1][0] else 1
        if (u, lot) not in met:
            met.add((u, lot))
            arrived(yb.at[u, pl.ds(*lots[lot])], sem_y + 2 * u + lot)
        return pf[u, zs[k], keep] + yb[u, k].astype(F32)

    def hop(u, way, step):
        return sem_z + 8 * u + way * 4 + step

    def z_first(u):
        chunk = partial(u, 0)
        for way, to in enumerate((zr, zl)):
            zsend[u, way, 0, :quarter] = chunk[way * quarter:(way + 1) * quarter]
            send(zsend.at[u, way, 0, pl.ds(0, quarter)], zrecv.at[u, way, 0, pl.ds(0, quarter)], dev(z_=to), hop(u, way, 0))

    def z_next(u, step):
        for way, to in enumerate((zr, zl)):
            chunk = partial(u, 2 * step - 1 + way)
            arrived(zrecv.at[u, way, step - 1, pl.ds(0, quarter if step == 1 else H)], hop(u, way, step - 1))
            if step == 1:
                zsend[u, way, step] = chunk
                rows = pl.ds(way * quarter, quarter)
                zsend[u, way, step, rows] = zsend[u, way, step, rows] + zrecv[u, way, 0, :quarter]
            else:
                zsend[u, way, step] = chunk + zrecv[u, way, step - 1]
            send(zsend.at[u, way, step], zrecv.at[u, way, step], dev(z_=to), hop(u, way, step))

    def z_last(u):
        total = partial(u, 7)
        for way in range(2):
            arrived(zrecv.at[u, way, 3], hop(u, way, 3))
            total = total + zrecv[u, way, 3]
        rfull[u, z, keep] = total.astype(BF16)

    a_last()
    own[0].wait()
    own[3].wait()
    g_go(0, 2)
    right(0, c)
    arrived(rbuf.at[yh * 2 + 1 - c], sem_rd)
    right(0, 1 - c)
    pair_sum(0)
    g_go(1, 1)
    for k in range(2):
        arrived(r_rows(rbuf.at[other], k), sem_r + k)
    send(rbuf.at[other], rbuf.at[other], sibling, sem_rd + 1)
    right(1, c)
    z_first(0)
    arrived(rbuf.at[(1 - yh) * 2 + 1 - c], sem_rd + 1)
    right(1, 1 - c)
    pair_sum(1)
    send(l_in, lbuf.at[mine], across, sem_l)
    g_go(1, 2)
    z_next(0, 1)
    b_first()
    send(bslot(xs[3], c), bslot(xs[3], c), sibling, sem_bd + 1)
    send(bslot(xs[1], c), bslot(xs[1], c), sibling, sem_bd + 2)
    g_go(0, 3)
    z_next(0, 2)
    z_first(1)
    g_go(1, 3)
    z_next(0, 3)
    z_next(1, 1)
    b_last()
    send(bslot(xs[2], c), bslot(xs[2], c), sibling, sem_bd + 3)

    own[1].wait()
    for k, xx in enumerate((x, xs[3], xs[1], xs[2])):
        arrived(bslot(xx, 1 - c), sem_bd + k)
    total = jnp.zeros((2 * T, E), F32)
    for j in range(8):
        total = total + jnp.dot(gbuf[j], bbuf[j], preferred_element_type=F32)
    prot[...] = total
    sem_rot, sem_xr = take(), take(3)
    send(prot.at[pl.ds((1 - yh) * T, T)], rprot, across, sem_rot)
    f0_begin, f0_go, f0_pair = relay(fslot(0), H)
    f1_begin, f1_go, f1_pair = relay(fslot(1), H)
    z_next(1, 2)
    z_last(0)
    f0_begin()
    z_next(1, 3)
    f0_go(0)
    arrived(lbuf.at[other], sem_l)
    send(lbuf.at[other], lbuf.at[other], sibling, sem_ld + 1)
    z_last(1)
    f1_begin()
    arrived(rprot, sem_rot)
    xrot[pl.ds(x * T, T)] = (prot[pl.ds(yh * T, T)] + rprot[...]).astype(BF16)
    for k in (1, 2, 3):
        send(xrot.at[pl.ds(x * T, T)], xrot.at[pl.ds(x * T, T)], dev(x_=xs[k]), sem_xr + k - 1)
    f0_go(1)
    f1_go(0)
    f0_go(2)
    f1_go(1)
    f0_go(3)
    f1_go(2)

    own[2].wait()
    arrived(lbuf.at[yh * 2 + 1 - c], sem_ld)
    arrived(lbuf.at[(1 - yh) * 2 + 1 - c], sem_ld + 1)
    for k in (1, 2, 3):
        arrived(xrot.at[pl.ds(xs[4 - k] * T, T)], sem_xr + k - 1)
        arrived(ends.at[xs[4 - k]], sem_e + k - 1)
    f1_go(3)
    for u in range(2):
        for cc in range(2):
            slot_of = (mine // 2 if u == 0 else other // 2) * 2 + cc
            part = jnp.dot(xrot[...], lbuf[slot_of], preferred_element_type=F32)
            for a in range(NX):
                left[u, 2 * a + cc] = part[a * T:(a + 1) * T]

    token = lax.broadcasted_iota(jnp.int32, (T, C), 0)

    def product(u, zz):
        prod = left[u, zz] * rfull[u, zz].astype(F32)
        stops = ends[zz // 2]
        below = [token < jnp.broadcast_to(stops[k:k + 1, :1], (T, C)) for k in range(SEQ_DEV)]
        rows = []
        for k in range(SEQ_DEV):
            inside = below[0] if k == 0 else below[k] & jnp.logical_not(below[k - 1])
            rows.append(jnp.sum(jnp.where(inside, prod, 0.0), axis=0, keepdims=True))
        at = (u * NZ + zz) * 8
        sbuf[pl.ds(pl.multiple_of(at, 8), 8)] = jnp.concatenate(rows + [jnp.zeros((8 - SEQ_DEV, C), F32)], axis=0)

    for k in range(-1, 4):
        for u, pair in enumerate((f0_pair, f1_pair)):
            pair(k)
            for far in {-1: (0,), 3: (4,)}.get(k, (k + 1, NZ - 1 - k)):
                product(u, (z + far) % NZ)

    sem_s = take(NM)
    column, query = (lax.broadcasted_iota(jnp.int32, (C, 128), k) for k in (0, 1))
    ranks = (column // RANK == query).astype(F32)
    tiles = jnp.dot(sbuf[...], ranks, precision=lax.Precision.HIGHEST, preferred_element_type=F32)
    finals = []
    for u in range(2):
        for zz in range(NZ):
            n = u * NZ + zz
            ssend[n] = tiles[n * 8:(n + 1) * 8]
            to_d, to_m = 4 * (zz // 2) + 2 * yh + c, 4 * x + (mine // 2 if u == 0 else other // 2) * 2 + zz % 2
            here = (to_d == d) & (to_m == m)
            cp = copy(ssend.at[n], srecv.at[m], (to_d, to_m), sem_s + n, sem_s + m)
            finals.append((here, cp))
            pl.when(jnp.logical_not(here))(cp.start)

            @pl.when(here)
            def _():
                srecv[m] = ssend[n]

    for src in range(NM):
        pl.when(jnp.logical_not((x == m // 4) & (m == src)))(functools.partial(arrived, srecv.at[src], sem_s + src))
    scores = srecv[0]
    for src in range(1, NM):
        scores = scores + srecv[src]
    scores = scores * (1.0 / jnp.sqrt(jnp.float32(RANK * TOK_DEV)))
    out[...] = scores[:SEQ_DEV, :C // RANK]

    for cp in sent:
        cp.wait_send()
    pl.when(moves)(lambda: move_g.wait_send())
    for here, cp in finals:
        pl.when(jnp.logical_not(here))(cp.wait_send)
    assert used[0] <= NSEM, used[0]


NSEM = 160


def on_device(out_grads, basis, left_factors, right_factors, activations, spans):
    vmem = pltpu.VMEM
    return pl.pallas_call(
        kernel,
        out_shape=jax.ShapeDtypeStruct((SEQ_DEV, C // RANK), F32),
        in_specs=[pl.BlockSpec(memory_space=pltpu.HBM)] * 5 + [pl.BlockSpec(memory_space=pltpu.SMEM)],
        out_specs=pl.BlockSpec(memory_space=vmem),
        scratch_shapes=[
            vmem((8, 2 * T, O), BF16),
            vmem((8, O, E), BF16),
            vmem((4, E, C), BF16),
            vmem((4, I, C), BF16),
            vmem((NX * T, I), BF16),
            vmem((2 * T, E), F32),
            vmem((T, E), F32),
            vmem((NX * T, E), BF16),
            vmem((2, NZ, T, C), F32),
            vmem((2, NZ, H, C), BF16),
            vmem((2, NZ, H, C), BF16),
            vmem((2, 2, 4, H, C), F32),
            vmem((2, 2, 4, H, C), F32),
            vmem((2, NZ, T, C), BF16),
            vmem((2, NZ, T, C), F32),
            vmem((NX, 8, 128), jnp.int32),
            vmem((NM * 8, C), F32),
            vmem((NM, 8, 128), F32),
            vmem((NM, 8, 128), F32),
            pltpu.SemaphoreType.DMA((5,)),
            pltpu.SemaphoreType.DMA((NSEM,)),
            pltpu.SemaphoreType.DMA((NSEM,)),
        ],
        compiler_params=pltpu.CompilerParams(collective_id=0, has_side_effects=True, vmem_limit_bytes=60 << 20),
    )(out_grads, basis, left_factors, right_factors, activations, spans)


def solution(mesh):
    placed = (
        P("dp", "mp"),
        P("dp", "mp"),
        P("mp", "dp"),
        P("mp", "dp"),
        P("dp", "mp"),
        P("dp", None),
    )
    return jax.shard_map(
        on_device, mesh=mesh, in_specs=placed, out_specs=P("dp", "mp"), check_vma=False
    )
```

time: 98.8 us -> 90.3 us (0.914)
  Pallas kernels: 96.8 us -> 89 us
    pallas_call x1, Pallas kernels: 96.8 us -> 89 us  [on_device(): pl.pallas_call(kernel, out_shape=jax.ShapeDtypeStruct((SEQ_DEV, C // RANK...]
where the time goes in v3:
time: 90.3 us; the launch traced here: 90.2 us
  Pallas kernels  89 us (99%)
  local copies, waits for them, and re-layouts  1.26 us (1%)
    pallas_call x1, Pallas kernels, on_device(): pl.pallas_call(kernel, out_shape=jax.ShapeDtypeStruct((SEQ_DEV, C // RANK...  89 us

profile of v3, /device:TPU:8, one launch (start us, length us, event | category | flops | bytes accessed | tf_op | source)
XLA Modules:
  0.0 90.2 jit_solution(11828290552124324366)
XLA Ops:
  0.0 89.0 %shard_map.64 = f32[4,8]{1,0:T(4,128)} custom-call(bf16[128,512]{1,0:T(8,128)(2,1)} %g_in.1, bf16[512,512]{1,0:T(8,128)(2,1)} %b_in.1, bf16[512,256]{1,0:T(8,128)(2,1)} %l_in.1, bf16[1792,256]{1,0:T(8,128)(2,1)} %r_in.1, bf16[128,1792]{1,0:T(8,128)(2,1)} %a_in.1, s32[1,5]{1,0:T(1,128)} %sp.1), custom_call_target="tpu_custom_call" | custom-call | tf_op jit(solution)/shard_map/pallas_call | solution.py:413
  89.0 1.3 %copy.8 = f32[4,8]{1,0:T(4,128)} copy(f32[4,8]{1,0:T(4,128)} %shard_map.64) | data formatting | bytes 256

commit v4 on v3

--- a/solution.py
+++ b/solution.py
@@ -121,17 +121,20 @@
             return slot(origin, 0, rows) if step < 4 else slot(origin, half * direction, half)
 
         def begin():
-            for direction, to in enumerate((zr, zl)):
-                send(slot(m), slot(m), dev(z_=to), sem + direction)
+            for far in (1, 2):
+                for direction in range(2):
+                    to = dev(z_=(z + (far, NZ - far)[direction]) % NZ)
+                    send(slot(m), slot(m), to, sem + 2 * (far - 1) + direction)
             send(slot(m), slot(m), beside, sem + 16)
 
         def go(k):
-            for direction, to in enumerate((zr, zl)):
+            for direction in range(2):
                 block = piece(yl, direction, k + 1)
                 arrived(block, sem + 2 * k + direction)
-                if k < 3:
-                    onward = block if k < 2 else slot(yl * NZ + (z + (-3, 3)[direction] + NZ) % NZ, half * direction, half)
-                    send(onward, onward, dev(z_=to), sem + 2 * (k + 1) + direction)
+                if k == 1:
+                    send(block, block, dev(z_=(zr, zl)[direction]), sem + 4 + direction)
+                    part = slot(yl * NZ + (z + (-2, 2)[direction] + NZ) % NZ, half * direction, half)
+                    send(part, part, dev(z_=(z + (2, NZ - 2)[direction]) % NZ), sem + 6 + direction)
                 send(block, block, beside, sem + 8 + 2 * k + direction)
 
         def pair(k):
@@ -178,7 +181,7 @@
     b_begin, b_first, b_last = ring(b_in, lambda xx, lo, n: bslot(xx, c, lo, n), O, (0, O // 4, O))
     sem_l, sem_rd, sem_ld, sem_bd = take(), take(2), take(2), take(4)
     sem_r = take(2)
-    r_cut = I // 4
+    r_cut = 640
     mine, other = yh * 2 + c, (1 - yh) * 2 + c
 
     def r_rows(slot, k):
@@ -224,11 +227,11 @@
             pf[u, 2 * a + cc] = part[a * T:(a + 1) * T]
 
     zs = [(z + k) % NZ for k in (4, 3, 5, 2, 6, 1, 7, 0)]
-    sem_y, sem_z = take(4), take(16)
+    sem_y, sem_z = take(6), take(16)
     quarter = H // 2
     keep, give = pl.ds(yl * H, H), pl.ds((1 - yl) * H, H)
 
-    lots = ((0, 3), (3, 5))
+    lots = ((0, 1), (1, 2), (3, 5))
     met = set()
 
     def pair_sum(u):
@@ -237,13 +240,13 @@
             for lot, (first, n) in enumerate(lots):
                 if k == first + n - 1:
                     blocks = pl.ds(first, n)
-                    send(pb.at[u, blocks], yb.at[u, blocks], beside, sem_y + 2 * u + lot)
+                    send(pb.at[u, blocks], yb.at[u, blocks], beside, sem_y + 3 * u + lot)
 
     def partial(u, k):
-        lot = 0 if k < lots[1][0] else 1
+        lot = max(i for i, (first, _) in enumerate(lots) if first <= k)
         if (u, lot) not in met:
             met.add((u, lot))
-            arrived(yb.at[u, pl.ds(*lots[lot])], sem_y + 2 * u + lot)
+            arrived(yb.at[u, pl.ds(*lots[lot])], sem_y + 3 * u + lot)
         return pf[u, zs[k], keep] + yb[u, k].astype(F32)
 
     def hop(u, way, step):
@@ -292,20 +295,23 @@
     right(1, 1 - c)
     pair_sum(1)
     send(l_in, lbuf.at[mine], across, sem_l)
-    g_go(1, 2)
-    z_next(0, 1)
     b_first()
     send(bslot(xs[3], c), bslot(xs[3], c), sibling, sem_bd + 1)
     send(bslot(xs[1], c), bslot(xs[1], c), sibling, sem_bd + 2)
-    g_go(0, 3)
+    g_go(1, 2)
+    z_next(0, 1)
+    z_first(1)
     z_next(0, 2)
-    z_first(1)
-    g_go(1, 3)
-    z_next(0, 3)
     z_next(1, 1)
     b_last()
     send(bslot(xs[2], c), bslot(xs[2], c), sibling, sem_bd + 3)
-
+    z_next(0, 3)
+    z_next(1, 2)
+    f0_begin, f0_go, f0_pair = relay(fslot(0), H)
+    f1_begin, f1_go, f1_pair = relay(fslot(1), H)
+
+    g_go(0, 3)
+    g_go(1, 3)
     own[1].wait()
     for k, xx in enumerate((x, xs[3], xs[1], xs[2])):
         arrived(bslot(xx, 1 - c), sem_bd + k)
@@ -313,37 +319,42 @@
     for j in range(8):
         total = total + jnp.dot(gbuf[j], bbuf[j], preferred_element_type=F32)
     prot[...] = total
-    sem_rot, sem_xr = take(), take(3)
-    send(prot.at[pl.ds((1 - yh) * T, T)], rprot, across, sem_rot)
-    f0_begin, f0_go, f0_pair = relay(fslot(0), H)
-    f1_begin, f1_go, f1_pair = relay(fslot(1), H)
-    z_next(1, 2)
+    sem_rot, sem_xr = take(2), take(6)
+    for p in range(2):
+        send(prot.at[pl.ds((1 - yh) * T + p * H, H)], rprot.at[pl.ds(p * H, H)], across, sem_rot + p)
+
+    def rotated(p):
+        arrived(rprot.at[pl.ds(p * H, H)], sem_rot + p)
+        at = pl.ds(x * T + p * H, H)
+        xrot[at] = (prot[pl.ds(yh * T + p * H, H)] + rprot[p * H:(p + 1) * H]).astype(BF16)
+        for k in (1, 2, 3):
+            send(xrot.at[at], xrot.at[at], dev(x_=xs[k]), sem_xr + 3 * p + k - 1)
+
+    z_next(1, 3)
     z_last(0)
     f0_begin()
-    z_next(1, 3)
+    z_last(1)
+    f1_begin()
     f0_go(0)
+    f0_go(1)
     arrived(lbuf.at[other], sem_l)
     send(lbuf.at[other], lbuf.at[other], sibling, sem_ld + 1)
-    z_last(1)
-    f1_begin()
-    arrived(rprot, sem_rot)
-    xrot[pl.ds(x * T, T)] = (prot[pl.ds(yh * T, T)] + rprot[...]).astype(BF16)
-    for k in (1, 2, 3):
-        send(xrot.at[pl.ds(x * T, T)], xrot.at[pl.ds(x * T, T)], dev(x_=xs[k]), sem_xr + k - 1)
-    f0_go(1)
+    rotated(0)
+    rotated(1)
     f1_go(0)
+    f1_go(1)
     f0_go(2)
-    f1_go(1)
     f0_go(3)
     f1_go(2)
+    f1_go(3)
 
     own[2].wait()
     arrived(lbuf.at[yh * 2 + 1 - c], sem_ld)
     arrived(lbuf.at[(1 - yh) * 2 + 1 - c], sem_ld + 1)
     for k in (1, 2, 3):
-        arrived(xrot.at[pl.ds(xs[4 - k] * T, T)], sem_xr + k - 1)
+        for p in range(2):
+            arrived(xrot.at[pl.ds(xs[4 - k] * T + p * H, H)], sem_xr + 3 * p + k - 1)
         arrived(ends.at[xs[4 - k]], sem_e + k - 1)
-    f1_go(3)
     for u in range(2):
         for cc in range(2):
             slot_of = (mine // 2 if u == 0 else other // 2) * 2 + cc
@@ -364,21 +375,19 @@
         at = (u * NZ + zz) * 8
         sbuf[pl.ds(pl.multiple_of(at, 8), 8)] = jnp.concatenate(rows + [jnp.zeros((8 - SEQ_DEV, C), F32)], axis=0)
 
-    for k in range(-1, 4):
-        for u, pair in enumerate((f0_pair, f1_pair)):
+    sem_s = take(NM)
+    column, query = (lax.broadcasted_iota(jnp.int32, (C, 128), k) for k in (0, 1))
+    ranks = (column // RANK == query).astype(F32)
+    finals = []
+    for u, pair in enumerate((f0_pair, f1_pair)):
+        for k in range(-1, 4):
             pair(k)
             for far in {-1: (0,), 3: (4,)}.get(k, (k + 1, NZ - 1 - k)):
                 product(u, (z + far) % NZ)
-
-    sem_s = take(NM)
-    column, query = (lax.broadcasted_iota(jnp.int32, (C, 128), k) for k in (0, 1))
-    ranks = (column // RANK == query).astype(F32)
-    tiles = jnp.dot(sbuf[...], ranks, precision=lax.Precision.HIGHEST, preferred_element_type=F32)
-    finals = []
-    for u in range(2):
+        tiles = jnp.dot(sbuf[u * 64:(u + 1) * 64], ranks, precision=lax.Precision.HIGHEST, preferred_element_type=F32)
         for zz in range(NZ):
             n = u * NZ + zz
-            ssend[n] = tiles[n * 8:(n + 1) * 8]
+            ssend[n] = tiles[zz * 8:(zz + 1) * 8]
             to_d, to_m = 4 * (zz // 2) + 2 * yh + c, 4 * x + (mine // 2 if u == 0 else other // 2) * 2 + zz % 2
             here = (to_d == d) & (to_m == m)
             cp = copy(ssend.at[n], srecv.at[m], (to_d, to_m), sem_s + n, sem_s + m)

time: 90.3 us -> 83.2 us (0.921); the launches traced: 90.2 us -> 82.1 us
  Pallas kernels: 89 us -> 80.8 us
    pallas_call x1, Pallas kernels: 89 us -> 80.8 us  [on_device(): pl.pallas_call(kernel, out_shape=jax.ShapeDtypeStruct((SEQ_DEV, C // RANK...]
where the time goes in v4:
time: 83.2 us; the launch traced here: 82.1 us
  Pallas kernels  80.8 us (97%)
  local copies, waits for them, and re-layouts  1.26 us (2%)
    pallas_call x1, Pallas kernels, on_device(): pl.pallas_call(kernel, out_shape=jax.ShapeDtypeStruct((SEQ_DEV, C // RANK...  80.8 us

profile of v4, /device:TPU:8, one launch (start us, length us, event | category | flops | bytes accessed | tf_op | source)
XLA Modules:
  0.0 82.1 jit_solution(7418802935088179321)
XLA Ops:
  0.0 80.8 %shard_map.64 = f32[4,8]{1,0:T(4,128)} custom-call(bf16[128,512]{1,0:T(8,128)(2,1)} %g_in.1, bf16[512,512]{1,0:T(8,128)(2,1)} %b_in.1, bf16[512,256]{1,0:T(8,128)(2,1)} %l_in.1, bf16[1792,256]{1,0:T(8,128)(2,1)} %r_in.1, bf16[128,1792]{1,0:T(8,128)(2,1)} %a_in.1, s32[1,5]{1,0:T(1,128)} %sp.1), custom_call_target="tpu_custom_call" | custom-call | tf_op jit(solution)/shard_map/pallas_call | solution.py:422
  80.8 1.3 %copy.8 = f32[4,8]{1,0:T(4,128)} copy(f32[4,8]{1,0:T(4,128)} %shard_map.64) | data formatting | bytes 256

commit v5 on v4

--- a/solution.py
+++ b/solution.py
@@ -179,7 +179,7 @@
 
     a_begin, a_first, a_last = ring(a_in, arow, T, (0, T))
     b_begin, b_first, b_last = ring(b_in, lambda xx, lo, n: bslot(xx, c, lo, n), O, (0, O // 4, O))
-    sem_l, sem_rd, sem_ld, sem_bd = take(), take(2), take(2), take(4)
+    sem_l, sem_rd, sem_ld, sem_bd = take(), take(3), take(2), take(4)
     sem_r = take(2)
     r_cut = 640
     mine, other = yh * 2 + c, (1 - yh) * 2 + c
@@ -189,6 +189,10 @@
 
     def r_send(k):
         send(r_rows(r_in, k), r_rows(rbuf.at[mine], k), across, sem_r + k)
+
+    def r_pass(k):
+        arrived(r_rows(rbuf.at[other], k), sem_r + k)
+        send(r_rows(rbuf.at[other], k), r_rows(rbuf.at[other], k), sibling, sem_rd + 1 + k)
 
     row = lax.broadcasted_iota(jnp.int32, (8, 128), 0)
     tile = jnp.zeros((8, 128), jnp.int32)
@@ -220,6 +224,7 @@
     b_begin(1)
     g_go(0, 1)
     g_go(1, 0)
+    r_pass(0)
 
     def right(u, cc):
         part = jnp.dot(abuf[...], rbuf[(mine // 2 if u == 0 else other // 2) * 2 + cc], preferred_element_type=F32)
@@ -286,12 +291,11 @@
     right(0, 1 - c)
     pair_sum(0)
     g_go(1, 1)
-    for k in range(2):
-        arrived(r_rows(rbuf.at[other], k), sem_r + k)
-    send(rbuf.at[other], rbuf.at[other], sibling, sem_rd + 1)
+    r_pass(1)
     right(1, c)
     z_first(0)
-    arrived(rbuf.at[(1 - yh) * 2 + 1 - c], sem_rd + 1)
+    for k in range(2):
+        arrived(r_rows(rbuf.at[(1 - yh) * 2 + 1 - c], k), sem_rd + 1 + k)
     right(1, 1 - c)
     pair_sum(1)
     send(l_in, lbuf.at[mine], across, sem_l)

time: 83.2 us -> 82.9 us (level)
  no operation moved by 1% of the time
where the time goes in v5:
time: 82.9 us; the launch traced here: 82.5 us
  Pallas kernels  81.2 us (98%)
  local copies, waits for them, and re-layouts  1.26 us (2%)
    pallas_call x1, Pallas kernels, on_device(): pl.pallas_call(kernel, out_shape=jax.ShapeDtypeStruct((SEQ_DEV, C // RANK...  81.2 us

profile of v5, /device:TPU:8, one launch (start us, length us, event | category | flops | bytes accessed | tf_op | source)
XLA Modules:
  0.0 82.5 jit_solution(10795471119411560774)
XLA Ops:
  0.0 81.2 %shard_map.64 = f32[4,8]{1,0:T(4,128)} custom-call(bf16[128,512]{1,0:T(8,128)(2,1)} %g_in.1, bf16[512,512]{1,0:T(8,128)(2,1)} %b_in.1, bf16[512,256]{1,0:T(8,128)(2,1)} %l_in.1, bf16[1792,256]{1,0:T(8,128)(2,1)} %r_in.1, bf16[128,1792]{1,0:T(8,128)(2,1)} %a_in.1, s32[1,5]{1,0:T(1,128)} %sp.1), custom_call_target="tpu_custom_call" | custom-call | tf_op jit(solution)/shard_map/pallas_call | solution.py:426
  81.2 1.3 %copy.8 = f32[4,8]{1,0:T(4,128)} copy(f32[4,8]{1,0:T(4,128)} %shard_map.64) | data formatting | bytes 256
